TPU v7x, 256 devices: a whole 4x4x8 slice. The times are simulated.
256 devices in a mesh: dp: 4 (over x), expert: 64 (over y, z, core).
Axes of the slice: x: 4, y: 4, z: 8, core: 2. Of those that a mesh axis runs over, the one named last changes fastest.
Arguments:
- stash_codes: bfloat16 [32768, 7168], P(('dp', 'expert')), may hold values from -6 to 6
- stash_scales: float32 [32768, 56], P(('dp', 'expert')), may hold values from 0.3 to 3
- expert_ids: int32 [32768, 8], P(('dp', 'expert')), may hold values from 0 to 255, as said below
- grad_rows: bfloat16 [256, 768, 1024], P(('dp', 'expert')), may hold values from -0.119628906 to 0.119628906
Outputs:
- weight_grad: bfloat16 [64, 7168, 1024], P(None, 'expert', 'dp')
Inputs may be any that keep to these rules, and one draw needn't show every extreme that they name: `expert_ids`: each row names 8 different experts. In the 128 rows of one device, an expert e with e % 4 == 0 is named by at most 12 rows; for each dp index, one such expert is named by exactly 12 rows on every device of that index.
All inputs are finite; a program needn't handle non-finite values.
Results may differ from a plain program's by a relative error of at most 0.022.
Values may be sent and summed in bfloat16 or wider, within the bound.
A program may use at most 128 MiB of HBM per device.

v0:
```python
import jax
import jax.numpy as jnp
from jax import lax
from jax.sharding import PartitionSpec as P

QB = 128
EXP_DEV = 4
CAP = 12


def hadamard(order):
    row_bits = jnp.arange(order, dtype=jnp.int32)[:, None]
    col_bits = jnp.arange(order, dtype=jnp.int32)[None, :]
    common = jnp.bitwise_and(row_bits, col_bits)
    parity = jnp.zeros((order, order), jnp.int32)
    for bit in range(order.bit_length() - 1):
        parity = parity + jnp.bitwise_and(jnp.right_shift(common, bit), 1)
    return (1 - 2 * (parity % 2)).astype(jnp.bfloat16)


def restore(codes, scales):
    row_count = codes.shape[0]
    block_count = codes.shape[1] // QB
    dequant = (
        codes.astype(jnp.float32).reshape(row_count, block_count, QB) * scales[:, :, None]
    ).astype(jnp.bfloat16)
    turned = jnp.dot(
        dequant.reshape(row_count * block_count, QB),
        hadamard(QB),
        preferred_element_type=jnp.float32,
    )
    return (turned * QB ** (-0.5)).astype(jnp.bfloat16).reshape(row_count, block_count * QB)


def slot_tables(routes, owners):
    targets = jnp.arange(owners, dtype=jnp.int32) * EXP_DEV
    member = jnp.any(routes[:, :, None] == targets[None, None, :], axis=1).astype(jnp.int32)
    ranking = jnp.cumsum(member, axis=0) - member
    slot_index = jnp.arange(CAP, dtype=jnp.int32)
    selector = member.T[:, None, :] * (ranking.T[:, None, :] == slot_index[None, :, None]).astype(
        jnp.int32
    )
    positions = jnp.arange(routes.shape[0], dtype=jnp.int32)
    source = jnp.sum(selector * positions[None, None, :], axis=2)
    filled = jnp.sum(selector, axis=2)
    return (source, filled)


def local(stash_codes, stash_scales, expert_ids, grad_rows):
    peer_count = lax.axis_size("expert")
    width = stash_codes.shape[1]
    source, filled = slot_tables(expert_ids, peer_count)
    flat_source = source.reshape(-1)
    kept_slots = filled.reshape(-1)
    codes_out = (
        jnp.take(stash_codes, flat_source, axis=0) * kept_slots.astype(jnp.bfloat16)[:, None]
    ).reshape(peer_count, CAP, width)
    scales_out = (
        jnp.take(stash_scales, flat_source, axis=0) * kept_slots.astype(jnp.float32)[:, None]
    ).reshape(peer_count, CAP, width // QB)
    codes_in, scales_in = (
        lax.all_to_all(codes_out, "expert", split_axis=0, concat_axis=0, tiled=True),
        lax.all_to_all(
            scales_out.astype(jnp.bfloat16), "expert", split_axis=0, concat_axis=0, tiled=True
        ).astype(scales_out.dtype),
    )
    arrived = restore(
        codes_in.reshape(peer_count * CAP, width), scales_in.reshape(peer_count * CAP, width // QB)
    )
    gradient = grad_rows[0]
    summed = lax.psum_scatter(
        lax.dot_general(
            gradient, arrived, (((0,), (0,)), ((), ())), preferred_element_type=jnp.float32
        ).astype(jnp.bfloat16),
        "dp",
        scatter_dimension=0,
        tiled=True,
    )
    turned_sum = summed.T[None]
    return lax.all_to_all(turned_sum, "expert", split_axis=1, concat_axis=0, tiled=True)


def solution(mesh):
    return jax.shard_map(
        local,
        mesh=mesh,
        in_specs=(
            P(("dp", "expert"), None),
            P(("dp", "expert"), None),
            P(("dp", "expert"), None),
            P(("dp", "expert"), None, None),
        ),
        out_specs=P(None, "expert", "dp"),
        check_vma=False,
    )
```

profile of v0, /device:TPU:1, one launch (start us, length us, event | category | flops | bytes accessed | tf_op | source)
XLA Modules:
  0.0 786.0 jit_solution(18072765396502428252)
XLA Ops:
  6.5 0.0 copy-start
  6.5 0.9 compare_reduce_fusion
  7.5 0.1 copy.23
  7.6 0.2 reduce_window_sum.13
  7.8 0.1 copy.24
  7.9 0.1 copy.25
  7.9 0.5 select_reduce_fusion
  8.4 0.1 copy.27
  8.5 0.1 reshape.92
  8.7 0.1 copy.26
  8.8 0.8 copy.30
  9.7 1.6 gather_fusion.1
  11.3 0.1 copy.31
  11.4 0.3 multiply_convert_fusion.2
  11.7 1.0 reshape.113
  12.7 13.2 %all-to-all-start.1 = ((bf16[64,2,336]{2,1,0:T(2,128)(2,1)}), bf16[64,2,336]{2,1,0:T(2,128)(2,1)S(1)}, u32[]{:S(2)}, u32[]{:S(2)}) async-start(bf16[64,2,336]{2,1,0:T(2,128)(2,1)} %reshape.113), calls=%async_computation.1 | async-start | bytes 196608 | tf_op jit(solution)/shard_map/all_to_all | solution.py:63
  25.9 0.0 copy-done
  25.9 9.4 %gather_fusion = bf16[768,7168]{1,0:T(8,128)(2,1)} fusion(bf16[128,7168]{1,0:T(8,128)(2,1)S(1)} %copy-done, s32[1024]{0:T(1024)S(1)} %pad_clamp_fusion), kind=kCustom, calls=%fused_computation | custom fusion | bytes 22023168 | tf_op jit(solution)/shard_map/jit(_take)/gather | solution.py:56
  35.3 15.3 %gather.13 = bf16[64,12,7168]{2,1,0:T(8,128)(2,1)} reshape(bf16[768,7168]{1,0:T(8,128)(2,1)} %gather_fusion) | data formatting | bytes 22020096 | tf_op jit(solution)/shard_map/jit(_take)/gather | solution.py:56
  50.6 0.1 copy.28
  50.7 11.0 %select_multiply_fusion = bf16[64,12,7168]{2,1,0:T(8,128)(2,1)} fusion(bf16[64,12,7168]{2,1,0:T(8,128)(2,1)} %gather.13, pred[64,12]{1,0:T(8,128)(4,1)S(1)} %copy.26, bf16[64,12]{1,0:T(8,128)(2,1)S(1)} %copy.28), kind=kLoop, calls=%fused_computation.6 | loop fusion | flops 11010048 | bytes 22022400 | tf_op jit(solution)/shard_map/mul | solution.py:56
  61.7 0.0 all-to-all-done.1
  61.7 10.5 %all-to-all-start = ((bf16[64,12,7168]{2,1,0:T(8,128)(2,1)}), bf16[64,12,7168]{2,1,0:T(8,128)(2,1)}, u32[]{:S(2)}, u32[]{:S(2)}) async-start(bf16[64,12,7168]{2,1,0:T(8,128)(2,1)} %select_multiply_fusion), calls=%async_computation | async-start | bytes 29360128 | tf_op jit(solution)/shard_map/all_to_all | solution.py:62
  72.2 0.0 reduce-scatter.2.cloned.1.call-start
  72.3 0.2 reshape.114
  72.5 0.3 reshape.95
  72.8 320.0 %all-to-all-done = bf16[64,12,7168]{2,1,0:T(8,128)(2,1)} async-done(((bf16[64,12,7168]{2,1,0:T(8,128)(2,1)}), bf16[64,12,7168]{2,1,0:T(8,128)(2,1)}, u32[]{:S(2)}, u32[]{:S(2)}) %all-to-all-start) | async-done | bytes 11010080 | tf_op jit(solution)/shard_map/all_to_all | solution.py:62
  392.9 22.7 %reshape.94 = f32[43008,128]{1,0:T(8,128)} reshape(bf16[64,12,7168]{2,1,0:T(8,128)(2,1)} %all-to-all-done) | data formatting | bytes 33030144 | tf_op jit(solution)/shard_map/convert_element_type | solution.py:25
  415.6 21.6 %fusion = bf16[43008,128]{1,0:T(8,128)(2,1)} fusion(f32[43008,128]{1,0:T(8,128)} %reshape.94, f32[43008]{0:T(1024)S(1)} %reshape.95), kind=kOutput, calls=%fused_computation.3 | convolution fusion | flops 1431879680 | bytes 33202176 | tf_op jit(solution)/shard_map/dot_general | solution.py:27
  437.2 0.0 copy-start.2
  437.2 16.6 %reshape.93 = bf16[768,7168]{1,0:T(8,128)(2,1)} reshape(bf16[43008,128]{1,0:T(8,128)(2,1)} %fusion) | data formatting | bytes 22020096 | tf_op jit(solution)/shard_map/reshape | solution.py:32
  453.8 0.0 copy-done.2
  453.8 18.6 %convert_bitcast_fusion = bf16[1024,7168]{0,1:T(8,128)(2,1)} fusion(bf16[768,7168]{1,0:T(8,128)(2,1)} %reshape.93, bf16[1,768,1024]{2,1,0:T(8,128)(2,1)S(1)} %copy-done.2), kind=kOutput, calls=%fused_computation.5 | convolution fusion | flops 11281629184 | bytes 27262976 | tf_op jit(solution)/shard_map/dot_general | solution.py:72
  472.4 0.0 reduce-scatter.2.cloned.1.call-update
  472.5 130.8 %reduce-scatter.2.cloned.1.call-done = bf16[256,7168]{0,1:T(8,128)(2,1)} async-done(((bf16[1024,7168]{0,1:T(8,128)(2,1)}), bf16[256,7168]{0,1:T(8,128)(2,1)}) %reduce-scatter.2.cloned.1.call-update) | async-done | bytes 3670032 | tf_op jit(solution)/shard_map/reduce_scatter | solution.py:71
  603.3 7.8 copy.35
  611.0 0.6 broadcast.79
  611.6 38.4 %reduce.2 = bf16[7168,256]{1,0:T(8,128)(2,1)} reduce(bf16[7168,1,256]{2,1,0:T(2,128)(2,1)} %bitcast.20, bf16[]{:T(256)} %broadcast.79), dimensions={1}, to_apply=%bitcast.19.reduce_sub_computation | reduce | bytes 7340034
  650.0 8.7 %reshape.115 = bf16[64,2,14336]{2,1,0:T(2,128)(2,1)} reshape(bf16[7168,256]{1,0:T(8,128)(2,1)} %reduce.2) | data formatting | bytes 7340032
  658.7 0.0 copy-start.1
  658.7 95.6 %all_to_all.22 = bf16[64,2,14336]{2,1,0:T(2,128)(2,1)} all-to-all(bf16[64,2,14336]{2,1,0:T(2,128)(2,1)} %reshape.115), channel_id=1, replica_groups=mesh['dp'=4,'expert'=64] {'expert'}, dimensions={0} | all-to-all | bytes 7340032 | tf_op jit(solution)/shard_map/all_to_all | solution.py:80
  754.3 19.3 %reshape.116 = bf16[7168,1,256]{2,1,0:T(2,128)(2,1)} reshape(bf16[64,2,14336]{2,1,0:T(2,128)(2,1)} %all_to_all.22) | data formatting | bytes 7340032
  773.6 5.5 copy.33
  779.2 0.0 copy-done.1
  (8 shorter events, 0.1 us)
Async XLA Ops:
  6.5 19.3 %copy-start = (bf16[128,7168]{1,0:T(8,128)(2,1)S(1)}, bf16[128,7168]{1,0:T(8,128)(2,1)}, u32[]{:S(2)}) copy-start(bf16[128,7168]{1,0:T(8,128)(2,1)} %param.4) | copy-start | bytes 5505028
  12.7 49.0 %all-to-all-start.1 = ((bf16[64,2,336]{2,1,0:T(2,128)(2,1)}), bf16[64,2,336]{2,1,0:T(2,128)(2,1)S(1)}, u32[]{:S(2)}, u32[]{:S(2)}) async-start(bf16[64,2,336]{2,1,0:T(2,128)(2,1)} %reshape.113), calls=%async_computation.1 | async-start | bytes 196608 | tf_op jit(solution)/shard_map/all_to_all | solution.py:63
  61.7 331.1 %all-to-all-start = ((bf16[64,12,7168]{2,1,0:T(8,128)(2,1)}), bf16[64,12,7168]{2,1,0:T(8,128)(2,1)}, u32[]{:S(2)}, u32[]{:S(2)}) async-start(bf16[64,12,7168]{2,1,0:T(8,128)(2,1)} %select_multiply_fusion), calls=%async_computation | async-start | bytes 29360128 | tf_op jit(solution)/shard_map/all_to_all | solution.py:62
  72.2 531.0 %reduce-scatter.2.cloned.1.call-start = ((), (), s32[]{:S(2)}) async-start(), calls=%async_computation.4 | async-start | bytes 18350080 | tf_op jit(solution)/shard_map/reduce_scatter | solution.py:71
  437.2 16.6 %copy-start.2 = (bf16[1,768,1024]{2,1,0:T(8,128)(2,1)S(1)}, bf16[1,768,1024]{2,1,0:T(8,128)(2,1)}, u32[]{:S(2)}) copy-start(bf16[1,768,1024]{2,1,0:T(8,128)(2,1)} %param.7) | copy-start | bytes 4718596
  658.7 120.5 %copy-start.1 = (bf16[128,7168]{1,0:T(8,128)(2,1)S(1)}, bf16[128,7168]{1,0:T(8,128)(2,1)}, u32[]{:S(2)}) copy-start(bf16[128,7168]{1,0:T(8,128)(2,1)} %param.4) | copy-start | bytes 5505028
Sparse Core Ops, SparseCore 0:
  472.6 130.6 reduce-scatter.1
where the time goes:
time: 789 us; the launch traced here: 786 us
  waiting for transfers between devices  451 us (57%)
  local copies, waits for them, and re-layouts  111 us (14%)
  blocking collectives  95.6 us (12%)
  other arithmetic  51.4 us (7%)
  matrix products  40.2 us (5%)
  starting transfers between devices  23.7 us (3%)
  between operations  13.5 us (2%)
    all_to_all x1, waiting for transfers between devices, local(): lax.all_to_all(codes_out, 'expert', split_axis=0, concat_axis=0, tiled=True)  320 us
    reduce_scatter x1, waiting for transfers between devices, local(): lax.psum_scatter(lax.dot_general(gradient, arrived, (((0,), (0,)), ((), (...  131 us
    all_to_all x1, blocking collectives, local(): lax.all_to_all(turned_sum, 'expert', split_axis=1, concat_axis=0, tiled=T...  95.6 us
    unnamed x1, other arithmetic  38.4 us
    unnamed x13, local copies, waits for them, and re-layouts  36.2 us
    gather x2, local copies, waits for them, and re-layouts, local(): jnp.take(stash_codes, flat_source, axis=0)  24.7 us
    convert_element_type x1, local copies, waits for them, and re-layouts, restore(): codes.astype(jnp.float32).reshape(row_count, block_count, QB)  22.7 us
    dot_general x1, matrix products, restore(): jnp.dot(dequant.reshape(row_count * block_count, QB), hadamard(QB), prefe...  21.6 us
  transfers between devices with their start and end apart: 3, of which 2 were waited for; matrix products, arithmetic and copies ran while one was open for 5% of the time, Pallas kernels for 0%

commit v1 on v0

v1 whole, which is shorter than its diff:
```python
import jax
import jax.numpy as jnp
from jax import lax
from jax.experimental import pallas as pl
from jax.experimental.pallas import tpu as pltpu
from jax.sharding import PartitionSpec as P

QB = 128
EXP_DEV = 4
CAP = 12
D = 7168
HW = 1024
TOK = 128
NX, NY, NZ = 4, 4, 8
RING = 2 * NZ
OWNERS = NY * RING
COLS = D // OWNERS
WIDTH = NY * COLS
SLOTS = OWNERS * CAP
HSH = HW // NX
TAB = 32
QUAD = 4
MESH = pl.DeviceIdType.MESH
BF16 = jnp.bfloat16
F32 = jnp.float32


def slot_table(routes):
    targets = jnp.arange(OWNERS, dtype=jnp.int32) * EXP_DEV
    member = jnp.any(routes[:, :, None] == targets[None, None, :], axis=1).astype(jnp.int32)
    ranking = jnp.cumsum(member, axis=0) - member
    slot_index = jnp.arange(CAP, dtype=jnp.int32)
    selector = member.T[:, None, :] * (ranking.T[:, None, :] == slot_index[None, :, None]).astype(
        jnp.int32
    )
    positions = jnp.arange(routes.shape[0], dtype=jnp.int32)
    token = jnp.sum(selector * (positions[None, None, :] + 1), axis=2) - 1
    token = token.reshape(NY, RING, 1, CAP)
    place = lax.axis_index("expert") % QUAD
    mine = (jnp.arange(QUAD, dtype=jnp.int32) == place)[None, None, :, None]
    spread = jnp.where(mine, token, -1).reshape(NY, RING * QUAD * CAP // 128, 128)
    spread = jnp.pad(spread, ((0, 0), (0, TAB // NY - spread.shape[1]), (0, 0)), constant_values=-1)
    return spread.reshape(TAB, 128).astype(BF16)


def rem(value, count):
    return lax.rem(value + count, count)


def kernel(
    codes, scales, table, grad, out, gbuf,
    send, tok, onehot, rows, gv, part, r1, r2, total,
    zs, zr, ys, yr, yfs, yfr, gs, gr, ss, sr, gl,
    s1s, s1r, s2s, s2r, cs, cr, cl, ol,
):
    x = lax.axis_index("dp")
    me = lax.axis_index("expert")
    y = lax.div(me, RING)
    zc = lax.rem(me, RING)
    z = lax.div(zc, 2)
    c = lax.rem(zc, 2)
    own = zc
    up_x, down_x = rem(x + 1, NX), rem(x - 1, NX)
    up_y, down_y = rem(y + 1, NY), rem(y - 1, NY)
    far_y = rem(y + 2, NY)
    up_z, down_z = rem(z + 1, NZ), rem(z - 1, NZ)
    dev_up_z = y * RING + 2 * up_z + c
    dev_down_z = y * RING + 2 * down_z + c
    sibling = y * RING + 2 * z + (1 - c)

    def rdma(src, dst, send_sem, recv_sem, dev_x, dev_e):
        return pltpu.make_async_remote_copy(
            src_ref=src, dst_ref=dst, send_sem=send_sem, recv_sem=recv_sem,
            device_id=(dev_x, dev_e), device_id_type=MESH,
        )

    barrier = pltpu.get_barrier_semaphore()
    for k in range(1, RING):
        pl.semaphore_signal(barrier, inc=1, device_id=(x, y * RING + rem(zc + k, RING)), device_id_type=MESH)
    for k in range(1, NY):
        pl.semaphore_signal(barrier, inc=1, device_id=(x, rem(y + k, NY) * RING + zc), device_id_type=MESH)
    for dev_x in (up_x, down_x):
        pl.semaphore_signal(barrier, inc=1, device_id=(dev_x, me), device_id_type=MESH)

    row_id = lax.broadcasted_iota(jnp.int32, (QB, QB), 0)
    col_id = lax.broadcasted_iota(jnp.int32, (QB, QB), 1)
    common = row_id & col_id
    parity = jnp.zeros((QB, QB), jnp.int32)
    for bit in range(7):
        parity = parity + ((common >> bit) & 1)
    had = (1 - 2 * (parity & 1)).astype(F32).astype(BF16)
    for k in range(D // QB):
        deq = (codes[:, k * QB:(k + 1) * QB].astype(F32) * scales[:, k:k + 1]).astype(BF16)
        turned = lax.dot_general(had, deq, (((1,), (1,)), ((), ())), preferred_element_type=F32)
        turned = (turned * QB ** (-0.5)).astype(BF16)
        start = 0
        while start < QB:
            n = k * QB + start
            idx, off = n // COLS, n % COLS
            length = min(QB - start, COLS - off)
            ty, tz = idx // RING, idx % RING
            send[tz, ty * COLS + off:ty * COLS + off + length, :] = turned[start:start + length]
            start += length
    for k in range(RING):
        send[k, WIDTH:WIDTH + TAB, :] = table[...]

    pl.semaphore_wait(barrier, RING - 1 + NY - 1 + 2)

    def z_copy(k, target, source):
        return rdma(
            send.at[target], tok.at[y * RING + source], zs.at[k], zr.at[k], x, y * RING + target
        )

    own_copy = pltpu.make_async_copy(send.at[own], tok.at[me], ol.at[0])
    own_copy.start()
    order = sorted(range(1, RING), key=lambda k: (min(k, RING - k), k))
    for k in order:
        z_copy(k, rem(zc + k, RING), zc).start()

    first_load = pltpu.make_async_copy(grad.at[0], gv.at[0], gl.at[0])
    first_load.start()

    def ring_z(j):
        return rem(z + (j + 1) // 2, NZ) if j % 2 else rem(z - j // 2, NZ)

    def piece(ref, j):
        if j == 7:
            return ref.at[pl.ds(SLOTS // 2, SLOTS // 2)]
        if j == 8:
            return ref.at[pl.ds(0, SLOTS // 2)]
        return ref

    def ring_copy(j, src, index):
        target = dev_down_z if j % 2 else dev_up_z
        return rdma(piece(src, j), piece(gbuf.at[index], j), gs.at[j], gr.at[j], x, target)

    def pair_copy(j, src, index):
        return rdma(piece(src, j), piece(gbuf.at[index], j), ss.at[j], sr.at[j], x, sibling)

    ring_copy(1, grad.at[0], own).start()
    ring_copy(2, grad.at[0], own).start()
    pair_copy(0, grad.at[0], own).start()

    def ring_step(j):
        index = 2 * ring_z(j) + c
        ring_copy(j, gbuf.at[index], index).wait_recv()
        if j <= 6:
            ring_copy(j + 2, gbuf.at[index], index).start()
        pair_copy(j, gbuf.at[index], index).start()

    def chunk(group, j):
        return tok.at[pl.ds(group * RING + 2 * ring_z(j), 2)]

    def y_copy(way, j, group, target):
        ref = chunk(group, j)
        return rdma(ref, ref, ys.at[way, j], yr.at[way, j], x, target * RING + zc)

    def far_copy(j, group):
        ref = chunk(group, j)
        target = down_y if j % 2 else up_y
        return rdma(ref, ref, yfs.at[j], yfr.at[j], x, target * RING + zc)

    for j in range(NZ):
        if j == 0:
            own_copy.wait()
            source = 2 * z + (1 - c)
            k = rem(zc - source, RING)
            z_copy(k, source, source).wait_recv()
        else:
            for core in range(2):
                source = 2 * ring_z(j) + core
                k = rem(zc - source, RING)
                z_copy(k, source, source).wait_recv()
        y_copy(0, j, y, up_y).start()
        y_copy(1, j, y, down_y).start()
    for j in range(NZ):
        y_copy(0, j, down_y, up_y).wait_recv()
        y_copy(1, j, up_y, down_y).wait_recv()
        far_copy(j, up_y if j % 2 else down_y).start()

    lane = lax.broadcasted_iota(jnp.int32, (128, 128), 1).astype(F32)

    def gather(q):
        for p in range(QUAD):
            words = tok[QUAD * q + p, WIDTH:WIDTH + TAB, :].astype(F32)
            each = TAB // NY
            mine = words[0:each]
            for group in range(1, NY):
                mine = jnp.where(y == group, words[group * each:(group + 1) * each], mine)
            for part_id in range(RING * QUAD * CAP // 128):
                column = jnp.broadcast_to(mine[part_id:part_id + 1, :], (128, 128)).T
                onehot[part_id * 128:(part_id + 1) * 128, p * 128:(p + 1) * 128] = jnp.where(
                    column == lane, 1.0, 0.0
                ).astype(BF16)
        blocks = jnp.concatenate([tok[QUAD * q + p, 0:WIDTH, :] for p in range(QUAD)], axis=1)
        picked = lax.dot_general(
            onehot[...], blocks, (((1,), (1,)), ((), ())), preferred_element_type=F32
        ).astype(BF16)
        height = QUAD * CAP
        for e in range(RING):
            rows[e, pl.ds(pl.multiple_of(q * height, height), height), :] = picked[
                e * height:(e + 1) * height
            ]

    quads = RING // QUAD

    def gather_step(step, carry):
        group = rem(y + lax.div(step, quads) - 1, NY)
        gather(group * quads + lax.rem(step, quads))
        return carry

    lax.fori_loop(0, 3 * quads, gather_step, 0)
    ring_step(1)
    ring_step(2)
    for j in range(NZ):
        far_copy(j, far_y).wait_recv()
    lax.fori_loop(3 * quads, 4 * quads, gather_step, 0)

    def place(i):
        j = lax.div(i, 2)
        half = lax.div(j + 1, 2)
        zj = rem(jnp.where(lax.rem(j, 2) == 1, z + half, z - half + NZ), NZ)
        core = rem(c + lax.rem(i, 2), 2)
        return 2 * zj + core

    def load(i):
        return pltpu.make_async_copy(gbuf.at[place(i)], gv.at[lax.rem(i, 2)], gl.at[lax.rem(i, 2)])

    half_rows = WIDTH // 2
    top, bottom = pl.ds(0, half_rows), pl.ds(half_rows, half_rows)
    opposite = rem(x + 2, NX)

    def first_copies(i):
        slot = lax.rem(i, 3)
        return (
            rdma(part.at[slot, opposite, top], r1.at[i, 0], s1s.at[i, 0], s1r.at[i, 0], up_x, me),
            rdma(part.at[slot, opposite, bottom], r1.at[i, 1], s1s.at[i, 1], s1r.at[i, 1], down_x, me),
        )

    def second_copies(i):
        slot = lax.rem(i, 3)
        return (
            rdma(part.at[slot, up_x], r2.at[i, 0], s2s.at[i, 0], s2r.at[i, 0], up_x, me),
            rdma(part.at[slot, down_x], r2.at[i, 1], s2s.at[i, 1], s2r.at[i, 1], down_x, me),
        )

    def out_copies(i):
        slot = lax.rem(i, 2)
        copies = []
        for k in range(1, NY):
            target = rem(y + k, NY)
            copies.append(rdma(
                total.at[slot, target], out.at[y * RING + place(i)],
                cs.at[i, k - 1], cr.at[i, k - 1], x, target * RING + zc,
            ))
        return copies

    def arrivals(i):
        slot = lax.rem(i, 2)
        return [
            rdma(
                total.at[slot, rem(y + k, NY)], out.at[rem(y - k, NY) * RING + place(i)],
                cs.at[i, k - 1], cr.at[i, k - 1], x, rem(y + k, NY) * RING + zc,
            )
            for k in range(1, NY)
        ]

    def own_out(i):
        slot = lax.rem(i, 2)
        return pltpu.make_async_copy(total.at[slot, y], out.at[y * RING + place(i)], cl.at[slot])

    def sent(i):
        for copy in first_copies(i):
            copy.wait_send()
        for copy in second_copies(i):
            copy.wait_send()

    def given(i):
        for copy in out_copies(i):
            copy.wait_send()
        own_out(i).wait()

    def main_step(i, carry):
        for at in (4, 8, 12):
            @pl.when(i == at)
            def _():
                ring_step(at // 2 + 1)
                ring_step(at // 2 + 2)

        @pl.when(i + 1 < RING)
        def _():
            j = lax.div(i + 1, 2)
            index = place(i + 1)

            @pl.when(jnp.logical_and(lax.rem(i, 2) == 0, j < NZ - 1))
            def _():
                rdma(gbuf.at[index], gbuf.at[index], ss.at[j], sr.at[j], x, sibling).wait_recv()

            @pl.when(jnp.logical_and(lax.rem(i, 2) == 0, j == NZ - 1))
            def _():
                for k in (7, 8):
                    pair_copy(k, gbuf.at[index], index).wait_recv()

            load(i + 1).start()

        @pl.when(i < RING)
        def _():
            slot, held = lax.rem(i, 3), lax.rem(i, 2)

            @pl.when(i >= 3)
            def _():
                sent(i - 3)

            pltpu.make_async_copy(grad.at[0], gv.at[held], gl.at[held]).wait()
            expert = place(i)
            for t in range(NX):
                part[slot, t] = lax.dot_general(
                    rows[expert], gv[held, :, t * HSH:(t + 1) * HSH],
                    (((0,), (0,)), ((), ())), preferred_element_type=F32,
                ).astype(BF16)
            for copy in first_copies(i):
                copy.start()

        @pl.when(jnp.logical_and(i >= 1, i < RING + 1))
        def _():
            b = i - 1
            slot = lax.rem(b, 3)
            for copy in first_copies(b):
                copy.wait_recv()
            part[slot, up_x, top] = (
                part[slot, up_x, top].astype(F32) + r1[b, 0].astype(F32)
            ).astype(BF16)
            part[slot, down_x, bottom] = (
                part[slot, down_x, bottom].astype(F32) + r1[b, 1].astype(F32)
            ).astype(BF16)
            for copy in second_copies(b):
                copy.start()

        @pl.when(i >= 2)
        def _():
            b = i - 2
            slot = lax.rem(b, 3)

            @pl.when(b >= 2)
            def _():
                given(b - 2)

            for copy in second_copies(b):
                copy.wait_recv()
            for group in range(NY):
                cut = pl.ds(group * COLS, COLS)
                total[lax.rem(b, 2), group] = (
                    part[slot, x, cut].astype(F32)
                    + r2[b, 0, cut].astype(F32)
                    + r2[b, 1, cut].astype(F32)
                ).astype(BF16)
            for copy in out_copies(b):
                copy.start()
            own_out(b).start()

        return carry

    lax.fori_loop(0, RING + 2, main_step, 0)

    def close(i, carry):
        for copy in arrivals(i):
            copy.wait_recv()
        return carry

    lax.fori_loop(0, RING, close, 0)
    for i in range(RING - 3, RING):
        sent(jnp.int32(i))
    for i in range(RING - 2, RING):
        given(jnp.int32(i))
    for k in range(1, RING):
        z_copy(k, rem(zc + k, RING), zc).wait_send()
    for j in range(NZ):
        y_copy(0, j, y, up_y).wait_send()
        y_copy(1, j, y, down_y).wait_send()
        far_copy(j, up_y if j % 2 else down_y).wait_send()
    for j in range(1, 9):
        ring_copy(j, grad.at[0], own).wait_send()
    for j in range(0, 9):
        pair_copy(j, grad.at[0], own).wait_send()


def local(stash_codes, stash_scales, expert_ids, grad_rows):
    table = slot_table(expert_ids)
    vmem = pl.BlockSpec(memory_space=pltpu.VMEM)
    hbm = pl.BlockSpec(memory_space=pl.ANY)
    dma = pltpu.SemaphoreType.DMA
    weight_grad, _ = pl.pallas_call(
        kernel,
        out_shape=(
            jax.ShapeDtypeStruct((OWNERS, COLS, HSH), BF16),
            jax.ShapeDtypeStruct((RING, SLOTS, HW), BF16),
        ),
        in_specs=[vmem, vmem, vmem, hbm],
        out_specs=(hbm, hbm),
        scratch_shapes=[
            pltpu.VMEM((RING, WIDTH + TAB, TOK), BF16),
            pltpu.VMEM((OWNERS, WIDTH + TAB, TOK), BF16),
            pltpu.VMEM((RING * QUAD * CAP, QUAD * TOK), BF16),
            pltpu.VMEM((RING, SLOTS, WIDTH), BF16),
            pltpu.VMEM((2, SLOTS, HW), BF16),
            pltpu.VMEM((3, NX, WIDTH, HSH), BF16),
            pltpu.VMEM((RING, 2, WIDTH // 2, HSH), BF16),
            pltpu.VMEM((RING, 2, WIDTH, HSH), BF16),
            pltpu.VMEM((2, NY, COLS, HSH), BF16),
            dma((RING,)), dma((RING,)),
            dma((2, NZ)), dma((2, NZ)), dma((NZ,)), dma((NZ,)),
            dma((9,)), dma((9,)), dma((9,)), dma((9,)), dma((2,)),
            dma((RING, 2)), dma((RING, 2)), dma((RING, 2)), dma((RING, 2)),
            dma((RING, 3)), dma((RING, 3)), dma((2,)), dma((1,)),
        ],
        compiler_params=pltpu.CompilerParams(
            collective_id=0, has_side_effects=True, vmem_limit_bytes=58 * 1024 * 1024
        ),
        cost_estimate=pl.CostEstimate(
            flops=2 * SLOTS * D * HW, bytes_accessed=100_000_000, transcendentals=0
        ),
    )(stash_codes, stash_scales, table, grad_rows)
    return weight_grad


def solution(mesh):
    return jax.shard_map(
        local,
        mesh=mesh,
        in_specs=(
            P(("dp", "expert"), None),
            P(("dp", "expert"), None),
            P(("dp", "expert"), None),
            P(("dp", "expert"), None, None),
        ),
        out_specs=P(None, "expert", "dp"),
        check_vma=False,
    )
```

time: 789 us -> 243 us (0.31)
  waiting for transfers between devices: 451 us -> 0 us
  Pallas kernels: 0 us -> 234 us
  local copies, waits for them, and re-layouts: 111 us -> 6.93 us
  blocking collectives: 95.6 us -> 0 us
  other arithmetic: 51.4 us -> 1.31 us
  matrix products: 40.2 us -> 0 us
  starting transfers between devices: 23.7 us -> 0 us
  between operations: 13.5 us -> 0.07 us
    all_to_all x2 -> x0, waiting for transfers between devices: 320 us -> none  [the longest x1 320 us: local(): lax.all_to_all(codes_out, 'expert', split_axis=0, concat_axis=0, tiled=True)]
    pallas_call x0 -> x1, Pallas kernels: none -> 234 us  [local(): pl.pallas_call(kernel, out_shape=(jax.ShapeDtypeStruct((OWNERS, COLS, HSH...]
    reduce_scatter x1 -> x0, waiting for transfers between devices: 131 us -> none  [local(): lax.psum_scatter(lax.dot_general(gradient, arrived, (((0,), (0,)), ((), (...]
    all_to_all x1 -> x0, blocking collectives: 95.6 us -> none  [local(): lax.all_to_all(turned_sum, 'expert', split_axis=1, concat_axis=0, tiled=T...]
    dot_general x2 -> x0, matrix products: 40.2 us -> none  [the longest x1 21.6 us: restore(): jnp.dot(dequant.reshape(row_count * block_count, QB), hadamard(QB), prefe...]
    unnamed x1 -> x0, other arithmetic: 38.4 us -> none
    unnamed x13 -> x2, local copies, waits for them, and re-layouts: 36.2 us -> 5.59 us
    gather x4 -> x0, local copies, waits for them, and re-layouts: 26.3 us -> none  [the longest x2 24.7 us: local(): jnp.take(stash_codes, flat_source, axis=0)]
  transfers between devices with their start and end apart: 3 -> 0, of which waited for: 2 -> 0; matrix products, arithmetic and copies ran while one was open for 5% -> 0% of each run, Pallas kernels for 0% -> 0%
where the time goes in v1:
time: 243 us; the launch traced here: 242 us
  Pallas kernels  234 us (96%)
  local copies, waits for them, and re-layouts  6.93 us (3%)
    pallas_call x1, Pallas kernels, local(): pl.pallas_call(kernel, out_shape=(jax.ShapeDtypeStruct((OWNERS, COLS, HSH...  234 us
    unnamed x2, local copies, waits for them, and re-layouts  5.59 us

profile of v1, /device:TPU:1, one launch (start us, length us, event | category | flops | bytes accessed | tf_op | source)
XLA Modules:
  0.0 242.4 jit_solution(9097190049673613880)
XLA Ops:
  0.0 0.8 compare_reduce_fusion
  0.8 0.1 broadcast_in_dim.33
  0.9 0.1 broadcast_in_dim.34
  1.0 0.1 copy.13
  1.1 1.5 copy.17.scales
  2.6 0.2 reduce_window_sum.13
  2.8 0.1 copy.14
  2.9 0.1 copy.15
  3.0 0.3 multiply_reduce_fusion
  3.3 0.1 copy.18
  3.4 0.2 broadcast_in_dim.37
  3.6 0.6 pad_bitcast_fusion.table
  4.2 234.1 %shard_map.46 = (bf16[64,112,256]{2,1,0:T(8,128)(2,1)}, bf16[16,768,1024]{2,1,0:T(8,128)(2,1)}) custom-call(bf16[128,7168]{1,0:T(8,128)(2,1)} %codes.1, f32[128,56]{1,0:T(8,128)} %copy.17.scales, bf16[32,128]{1,0:T(8,128)(2,1)} %pad_bitcast_fusion.table, bf16[1,768,1024]{2,1,0:T(8,128)(2,1)} %grad.1), custom_call_target="tpu_custom_call" | custom-call | flops 11274289152 | bytes 100000000 | tf_op jit(solution)/shard_map/pallas_call | solution.py:392
  238.3 4.1 %copy.20 = bf16[64,112,256]{2,1,0:T(8,128)(2,1)} copy(bf16[64,112,256]{2,1,0:T(8,128)(2,1)} %get-tuple-element.6) | data formatting | bytes 7340032
  (8 shorter events, 0.1 us)

commit v2 on v0

v2 whole, which is shorter than its diff:
```python
import jax
import jax.numpy as jnp
from jax import lax
from jax.experimental import pallas as pl
from jax.experimental.pallas import tpu as pltpu
from jax.sharding import PartitionSpec as P

QB = 128
EXP_DEV = 4
CAP = 12
D = 7168
HW = 1024
TOK = 128
NX, NY, NZ = 4, 4, 8
RING = 2 * NZ
OWNERS = NY * RING
COLS = D // OWNERS
WIDTH = NY * COLS
SLOTS = OWNERS * CAP
HSH = HW // NX
TAB = 32
HALVES = 2
PART = WIDTH // HALVES
UNITS = RING * HALVES
DEPTH = 6
KEEP = 4
CUTS = 4
QUAD = 4
MESH = pl.DeviceIdType.MESH
BF16 = jnp.bfloat16
F32 = jnp.float32


def slot_table(routes):
    targets = jnp.arange(OWNERS, dtype=jnp.int32) * EXP_DEV
    member = jnp.any(routes[:, :, None] == targets[None, None, :], axis=1).astype(jnp.int32)
    ranking = jnp.cumsum(member, axis=0) - member
    slot_index = jnp.arange(CAP, dtype=jnp.int32)
    selector = member.T[:, None, :] * (ranking.T[:, None, :] == slot_index[None, :, None]).astype(
        jnp.int32
    )
    positions = jnp.arange(routes.shape[0], dtype=jnp.int32)
    token = jnp.sum(selector * (positions[None, None, :] + 1), axis=2) - 1
    token = token.reshape(NY, RING, 1, CAP)
    place = lax.axis_index("expert") % QUAD
    mine = (jnp.arange(QUAD, dtype=jnp.int32) == place)[None, None, :, None]
    spread = jnp.where(mine, token, -1).reshape(NY, RING * QUAD * CAP // 128, 128)
    spread = jnp.pad(spread, ((0, 0), (0, TAB // NY - spread.shape[1]), (0, 0)), constant_values=-1)
    return spread.reshape(TAB, 128).astype(BF16)


def rem(value, count):
    return lax.rem(value + count, count)


def kernel(
    codes, scales, table, grad, out, gbuf,
    code, send0, send1, tok0, tok1, onehot, rows, gv, part, r1, r2, total,
    il, ol, zs, zr, ys, yr, yfs, yfr, gs, gr, ss, sr, gl,
    s1s, s1r, s2s, s2r, cs, cr, cl,
):
    x = lax.axis_index("dp")
    me = lax.axis_index("expert")
    y = lax.div(me, RING)
    zc = lax.rem(me, RING)
    z = lax.div(zc, 2)
    c = lax.rem(zc, 2)
    own = zc
    up_x, down_x = rem(x + 1, NX), rem(x - 1, NX)
    up_y, down_y = rem(y + 1, NY), rem(y - 1, NY)
    far_y = rem(y + 2, NY)
    dev_up_z = y * RING + 2 * rem(z + 1, NZ) + c
    dev_down_z = y * RING + 2 * rem(z - 1, NZ) + c
    sibling = y * RING + 2 * z + (1 - c)
    send, tok = (send0, send1), (tok0, tok1)

    def rdma(src, dst, send_sem, recv_sem, dev_x, dev_e):
        return pltpu.make_async_remote_copy(
            src_ref=src, dst_ref=dst, send_sem=send_sem, recv_sem=recv_sem,
            device_id=(dev_x, dev_e), device_id_type=MESH,
        )

    step = D // CUTS
    fetches = [
        pltpu.make_async_copy(
            codes.at[:, pl.ds(k * step, step)], code.at[:, pl.ds(k * step, step)], il.at[k]
        )
        for k in range(CUTS)
    ]
    for fetch in fetches:
        fetch.start()

    barrier = pltpu.get_barrier_semaphore()
    for k in range(1, RING):
        pl.semaphore_signal(barrier, inc=1, device_id=(x, y * RING + rem(zc + k, RING)), device_id_type=MESH)
    for k in range(1, NY):
        pl.semaphore_signal(barrier, inc=1, device_id=(x, rem(y + k, NY) * RING + zc), device_id_type=MESH)
    for dev_x in (up_x, down_x):
        pl.semaphore_signal(barrier, inc=1, device_id=(dev_x, me), device_id_type=MESH)

    row_id = lax.broadcasted_iota(jnp.int32, (QB, QB), 0)
    col_id = lax.broadcasted_iota(jnp.int32, (QB, QB), 1)
    common = row_id & col_id
    parity = jnp.zeros((QB, QB), jnp.int32)
    for bit in range(7):
        parity = parity + ((common >> bit) & 1)
    had = (1 - 2 * (parity & 1)).astype(F32).astype(BF16)

    def restore(half):
        blocks = D // QB // HALVES
        for k in range(half * blocks, (half + 1) * blocks):
            if k % (D // QB // CUTS) == 0:
                fetches[k // (D // QB // CUTS)].wait()
            turned = lax.dot_general(
                had, code[:, k * QB:(k + 1) * QB], (((1,), (1,)), ((), ())), preferred_element_type=F32
            )
            turned = (turned * (scales[k:k + 1, :] * QB ** (-0.5))).astype(BF16)
            start = 0
            while start < QB:
                n = k * QB + start
                idx, off = n // COLS, n % COLS
                length = min(QB - start, COLS - off)
                ty, tz = idx // RING, idx % RING
                at = (ty - half * (NY // HALVES)) * COLS + off
                send[half][tz, at:at + length, :] = turned[start:start + length]
                start += length

    def z_copy(half, k, target, source):
        return rdma(
            send[half].at[target], tok[half].at[y * RING + source],
            zs.at[half, k], zr.at[half, k], x, y * RING + target,
        )

    own_copies = [
        pltpu.make_async_copy(send[half].at[own], tok[half].at[me], ol.at[half]) for half in range(HALVES)
    ]
    order = sorted(range(1, RING), key=lambda k: (min(k, RING - k), k))
    for k in range(RING):
        send0[k, PART:PART + TAB, :] = table[...]
    for half in range(HALVES):
        restore(half)
        if half == 0:
            pl.semaphore_wait(barrier, RING - 1 + NY - 1 + 2)
        for k in order:
            z_copy(half, k, rem(zc + k, RING), zc).start()
        own_copies[half].start()

    first_load = pltpu.make_async_copy(grad.at[0], gv.at[0], gl.at[0])
    first_load.start()

    def ring_z(j):
        return rem(z + (j + 1) // 2, NZ) if j % 2 else rem(z - j // 2, NZ)

    def cut(ref, h):
        return ref.at[pl.ds(h * (SLOTS // 2), SLOTS // 2)]

    def ring_copy(j, h, src, index):
        target = dev_down_z if j % 2 else dev_up_z
        return rdma(cut(src, h), cut(gbuf.at[index], h), gs.at[j, h], gr.at[j, h], x, target)

    def pair_copy(j, h, src, index):
        return rdma(cut(src, h), cut(gbuf.at[index], h), ss.at[j, h], sr.at[j, h], x, sibling)

    def holds(j, h):
        return not (j == 7 and h == 0 or j == 8 and h == 1)

    for h in range(2):
        ring_copy(1, h, grad.at[0], own).start()
        ring_copy(2, h, grad.at[0], own).start()
        pair_copy(0, h, grad.at[0], own).start()

    def ring_step(distance, h):
        for j in (2 * distance - 1, 2 * distance):
            if holds(j, h):
                index = 2 * ring_z(j) + c
                ring_copy(j, h, gbuf.at[index], index).wait_recv()
                if j <= 6 and holds(j + 2, h):
                    ring_copy(j + 2, h, gbuf.at[index], index).start()
                pair_copy(j, h, gbuf.at[index], index).start()

    def chunk(half, group, j):
        return tok[half].at[pl.ds(group * RING + 2 * ring_z(j), 2)]

    def y_copy(half, way, j, group, target):
        ref = chunk(half, group, j)
        return rdma(ref, ref, ys.at[half, way, j], yr.at[half, way, j], x, target * RING + zc)

    def far_copy(half, j, group):
        ref = chunk(half, group, j)
        target = down_y if j % 2 else up_y
        return rdma(ref, ref, yfs.at[half, j], yfr.at[half, j], x, target * RING + zc)

    def spread_y(half):
        for j in range(NZ):
            if j == 0:
                own_copies[half].wait()
            for source in ([2 * z + (1 - c)] if j == 0 else [2 * ring_z(j), 2 * ring_z(j) + 1]):
                z_copy(half, rem(zc - source, RING), source, source).wait_recv()
            y_copy(half, 0, j, y, up_y).start()
            y_copy(half, 1, j, y, down_y).start()

    def pass_y(half, first, last):
        for j in range(first, last):
            y_copy(half, 0, j, down_y, up_y).wait_recv()
            y_copy(half, 1, j, up_y, down_y).wait_recv()
            far_copy(half, j, up_y if j % 2 else down_y).start()

    lane = lax.broadcasted_iota(jnp.int32, (128, 128), 1).astype(F32)

    def gather(half, q):
        for p in range(QUAD):
            words = tok0[QUAD * q + p, PART:PART + TAB, :].astype(F32)
            each = TAB // NY
            mine = words[0:each]
            for group in range(1, NY):
                mine = jnp.where(y == group, words[group * each:(group + 1) * each], mine)
            for part_id in range(RING * QUAD * CAP // 128):
                column = jnp.broadcast_to(mine[part_id:part_id + 1, :], (128, 128)).T
                onehot[part_id * 128:(part_id + 1) * 128, p * 128:(p + 1) * 128] = jnp.where(
                    column == lane, 1.0, 0.0
                ).astype(BF16)
        blocks = jnp.concatenate([tok[half][QUAD * q + p, 0:PART, :] for p in range(QUAD)], axis=1)
        picked = lax.dot_general(
            onehot[...], blocks, (((1,), (1,)), ((), ())), preferred_element_type=F32
        ).astype(BF16)
        height = QUAD * CAP
        for e in range(RING):
            rows[half, e, pl.ds(pl.multiple_of(q * height, height), height), :] = picked[
                e * height:(e + 1) * height
            ]

    quads = RING // QUAD

    def gather_some(half, first, last):
        def body(step, carry):
            group = rem(y + lax.div(step, quads) - 1, NY)
            gather(half, group * quads + lax.rem(step, quads))
            return carry

        lax.fori_loop(first, last, body, 0)

    def place(i):
        j = lax.div(i, 2)
        half = lax.div(j + 1, 2)
        zj = rem(jnp.where(lax.rem(j, 2) == 1, z + half, z - half + NZ), NZ)
        core = rem(c + lax.rem(i, 2), 2)
        return 2 * zj + core

    def unit(u):
        i = jnp.where(u < 4, lax.rem(u, 2), lax.div(u, 2))
        half = jnp.where(u < 4, lax.div(u, 2), lax.rem(u, 2))
        return i, half

    def load(i):
        return pltpu.make_async_copy(gbuf.at[place(i)], gv.at[lax.rem(i, 2)], gl.at[lax.rem(i, 2)])

    def bring(i):
        j = lax.div(i, 2)
        index = place(i)
        other = lax.rem(i, 2) == 1
        for h in range(2):
            @pl.when(jnp.logical_and(other, j < NZ - 1))
            def _():
                ref = cut(gbuf.at[index], h)
                rdma(ref, ref, ss.at[j, h], sr.at[j, h], x, sibling).wait_recv()

            @pl.when(jnp.logical_and(other, j == NZ - 1))
            def _():
                pair_copy(8 - h, h, gbuf.at[index], index).wait_recv()

        load(i).start()

    mid = PART // 2
    top, bottom = pl.ds(0, mid), pl.ds(mid, mid)
    opposite = rem(x + 2, NX)

    def first_copies(u):
        slot = lax.rem(u, DEPTH)
        return (
            rdma(part.at[slot, opposite, top], r1.at[u, 0], s1s.at[u, 0], s1r.at[u, 0], up_x, me),
            rdma(part.at[slot, opposite, bottom], r1.at[u, 1], s1s.at[u, 1], s1r.at[u, 1], down_x, me),
        )

    def second_copies(u):
        slot = lax.rem(u, DEPTH)
        return (
            rdma(part.at[slot, up_x], r2.at[u, 0], s2s.at[u, 0], s2r.at[u, 0], up_x, me),
            rdma(part.at[slot, down_x], r2.at[u, 1], s2s.at[u, 1], s2r.at[u, 1], down_x, me),
        )

    def sent(u):
        for copy in first_copies(u):
            copy.wait_send()
        for copy in second_copies(u):
            copy.wait_send()

    def out_copies(u, remote, local):
        i, half = unit(u)
        slot = lax.rem(u, KEEP)
        for k in range(NY // HALVES):
            target = half * (NY // HALVES) + k
            away = rem(target - y, NY)

            @pl.when(away != 0)
            def _():
                remote(rdma(
                    total.at[slot, k], out.at[y * RING + place(i)],
                    cs.at[slot, k], cr.at[i, away], x, target * RING + zc,
                ))

            @pl.when(away == 0)
            def _():
                local(pltpu.make_async_copy(total.at[slot, k], out.at[y * RING + place(i)], cl.at[slot]))

    def give(u):
        out_copies(u, lambda copy: copy.start(), lambda copy: copy.start())

    def given(u):
        out_copies(u, lambda copy: copy.wait_send(), lambda copy: copy.wait())

    def multiply(u):
        i, half = unit(u)
        slot, held = lax.rem(u, DEPTH), lax.rem(i, 2)
        expert = place(i)

        @pl.when(u >= DEPTH)
        def _():
            sent(u - DEPTH)

        @pl.when(jnp.logical_or(u < 2, jnp.logical_and(u >= 4, lax.rem(u, 2) == 0)))
        def _():
            pltpu.make_async_copy(grad.at[0], gv.at[held], gl.at[held]).wait()

        for t in range(NX):
            part[slot, t] = lax.dot_general(
                rows[half, expert], gv[held, :, t * HSH:(t + 1) * HSH],
                (((0,), (0,)), ((), ())), preferred_element_type=F32,
            ).astype(BF16)
        for copy in first_copies(u):
            copy.start()

    def combine(u):
        slot = lax.rem(u, DEPTH)
        for copy in first_copies(u):
            copy.wait_recv()
        part[slot, up_x, top] = (
            part[slot, up_x, top].astype(F32) + r1[u, 0].astype(F32)
        ).astype(BF16)
        part[slot, down_x, bottom] = (
            part[slot, down_x, bottom].astype(F32) + r1[u, 1].astype(F32)
        ).astype(BF16)
        for copy in second_copies(u):
            copy.start()

    def finish(u):
        slot = lax.rem(u, DEPTH)

        @pl.when(u >= KEEP)
        def _():
            given(u - KEEP)

        for copy in second_copies(u):
            copy.wait_recv()
        for k in range(NY // HALVES):
            span = pl.ds(k * COLS, COLS)
            total[lax.rem(u, KEEP), k] = (
                part[slot, x, span].astype(F32)
                + r2[u, 0, span].astype(F32)
                + r2[u, 1, span].astype(F32)
            ).astype(BF16)
        give(u)

    def repeat(function):
        def body(u, carry):
            function(u)
            return carry

        lax.fori_loop(0, 2, body, 0)

    spread_y(0)
    pass_y(0, 0, NZ)
    spread_y(1)
    gather_some(0, 0, 3 * quads)
    for j in range(NZ):
        far_copy(0, j, far_y).wait_recv()
    gather_some(0, 3 * quads, 4 * quads)
    bring(jnp.int32(1))
    repeat(multiply)
    pass_y(1, 0, NZ // 2)
    repeat(combine)
    pass_y(1, NZ // 2, NZ)
    repeat(finish)
    gather_some(1, 0, 3 * quads)
    ring_step(1, 0)
    for j in range(NZ):
        far_copy(1, j, far_y).wait_recv()
    gather_some(1, 3 * quads, 4 * quads)

    def main_step(u, carry):
        following = lax.div(u, 2) + 1
        due = jnp.logical_and(lax.rem(u, 2) == 1, following < RING)
        fresh = lax.rem(following, 4) == 2

        @pl.when(jnp.logical_and(due, jnp.logical_not(fresh)))
        def _():
            bring(following)

        @pl.when(u < UNITS)
        def _():
            multiply(u)

        @pl.when(jnp.logical_and(u >= 4, u < UNITS + 2))
        def _():
            combine(u - 2)

        @pl.when(u >= 6)
        def _():
            finish(u - 4)

        for at, distance, h in ((3, 1, 1), (9, 2, 0), (11, 2, 1), (17, 3, 0), (19, 3, 1), (26, 4, 0), (27, 4, 1)):
            @pl.when(u == at)
            def _():
                ring_step(distance, h)

        @pl.when(jnp.logical_and(due, fresh))
        def _():
            bring(following)

        return carry

    lax.fori_loop(2, UNITS + 4, main_step, 0)

    def close(i, carry):
        for k in range(1, NY):
            source = rem(y - k, NY)
            rdma(
                total.at[0, 0], out.at[source * RING + place(i)],
                cs.at[0, 0], cr.at[i, k], x, source * RING + zc,
            ).wait_recv()
        return carry

    lax.fori_loop(0, RING, close, 0)

    def close_units(u, carry):
        sent(u)
        return carry

    def close_outs(u, carry):
        given(u)
        return carry

    lax.fori_loop(UNITS - DEPTH, UNITS, close_units, 0)
    lax.fori_loop(UNITS - KEEP, UNITS, close_outs, 0)
    for half in range(HALVES):
        for k in range(1, RING):
            z_copy(half, k, rem(zc + k, RING), zc).wait_send()
        for j in range(NZ):
            y_copy(half, 0, j, y, up_y).wait_send()
            y_copy(half, 1, j, y, down_y).wait_send()
            far_copy(half, j, up_y if j % 2 else down_y).wait_send()
    for j in range(0, 9):
        for h in range(2):
            if holds(j, h):
                if j > 0:
                    ring_copy(j, h, grad.at[0], own).wait_send()
                pair_copy(j, h, grad.at[0], own).wait_send()


def local(stash_codes, stash_scales, expert_ids, grad_rows):
    table = slot_table(expert_ids)
    vmem = pl.BlockSpec(memory_space=pltpu.VMEM)
    hbm = pl.BlockSpec(memory_space=pl.ANY)
    dma = pltpu.SemaphoreType.DMA
    weight_grad, _ = pl.pallas_call(
        kernel,
        out_shape=(
            jax.ShapeDtypeStruct((OWNERS, COLS, HSH), BF16),
            jax.ShapeDtypeStruct((RING, SLOTS, HW), BF16),
        ),
        in_specs=[hbm, vmem, vmem, hbm],
        out_specs=(hbm, hbm),
        scratch_shapes=[
            pltpu.VMEM((TOK, D), BF16),
            pltpu.VMEM((RING, PART + TAB, TOK), BF16),
            pltpu.VMEM((RING, PART, TOK), BF16),
            pltpu.VMEM((OWNERS, PART + TAB, TOK), BF16),
            pltpu.VMEM((OWNERS, PART, TOK), BF16),
            pltpu.VMEM((RING * QUAD * CAP, QUAD * TOK), BF16),
            pltpu.VMEM((HALVES, RING, SLOTS, PART), BF16),
            pltpu.VMEM((2, SLOTS, HW), BF16),
            pltpu.VMEM((DEPTH, NX, PART, HSH), BF16),
            pltpu.VMEM((UNITS, 2, PART // 2, HSH), BF16),
            pltpu.VMEM((UNITS, 2, PART, HSH), BF16),
            pltpu.VMEM((KEEP, NY // HALVES, COLS, HSH), BF16),
            dma((CUTS,)), dma((HALVES,)),
            dma((HALVES, RING)), dma((HALVES, RING)),
            dma((HALVES, 2, NZ)), dma((HALVES, 2, NZ)), dma((HALVES, NZ)), dma((HALVES, NZ)),
            dma((9, 2)), dma((9, 2)), dma((9, 2)), dma((9, 2)), dma((2,)),
            dma((UNITS, 2)), dma((UNITS, 2)), dma((UNITS, 2)), dma((UNITS, 2)),
            dma((KEEP, 2)), dma((RING, NY)), dma((KEEP,)),
        ],
        compiler_params=pltpu.CompilerParams(
            collective_id=0, has_side_effects=True, vmem_limit_bytes=58 * 1024 * 1024
        ),
        cost_estimate=pl.CostEstimate(
            flops=2 * SLOTS * D * HW, bytes_accessed=100_000_000, transcendentals=0
        ),
    )(stash_codes, stash_scales.T, table, grad_rows)
    return weight_grad


def solution(mesh):
    return jax.shard_map(
        local,
        mesh=mesh,
        in_specs=(
            P(("dp", "expert"), None),
            P(("dp", "expert"), None),
            P(("dp", "expert"), None),
            P(("dp", "expert"), None, None),
        ),
        out_specs=P(None, "expert", "dp"),
        check_vma=False,
    )
```

time: 789 us -> 225 us (0.29)
  waiting for transfers between devices: 451 us -> 0 us
  Pallas kernels: 0 us -> 215 us
  local copies, waits for them, and re-layouts: 111 us -> 5.45 us
  blocking collectives: 95.6 us -> 0 us
  other arithmetic: 51.4 us -> 1.31 us
  matrix products: 40.2 us -> 0 us
  starting transfers between devices: 23.7 us -> 0 us
  between operations: 13.5 us -> 0.07 us
    all_to_all x2 -> x0, waiting for transfers between devices: 320 us -> none  [the longest x1 320 us: local(): lax.all_to_all(codes_out, 'expert', split_axis=0, concat_axis=0, tiled=True)]
    pallas_call x0 -> x1, Pallas kernels: none -> 215 us  [local(): pl.pallas_call(kernel, out_shape=(jax.ShapeDtypeStruct((OWNERS, COLS, HSH...]
    reduce_scatter x1 -> x0, waiting for transfers between devices: 131 us -> none  [local(): lax.psum_scatter(lax.dot_general(gradient, arrived, (((0,), (0,)), ((), (...]
    all_to_all x1 -> x0, blocking collectives: 95.6 us -> none  [local(): lax.all_to_all(turned_sum, 'expert', split_axis=1, concat_axis=0, tiled=T...]
    dot_general x2 -> x0, matrix products: 40.2 us -> none  [the longest x1 21.6 us: restore(): jnp.dot(dequant.reshape(row_count * block_count, QB), hadamard(QB), prefe...]
    unnamed x1 -> x0, other arithmetic: 38.4 us -> none
    unnamed x13 -> x1, local copies, waits for them, and re-layouts: 36.2 us -> 4.11 us
    gather x4 -> x0, local copies, waits for them, and re-layouts: 26.3 us -> none  [the longest x2 24.7 us: local(): jnp.take(stash_codes, flat_source, axis=0)]
  transfers between devices with their start and end apart: 3 -> 0, of which waited for: 2 -> 0; matrix products, arithmetic and copies ran while one was open for 5% -> 0% of each run, Pallas kernels for 0% -> 0%
where the time goes in v2:
time: 225 us; the launch traced here: 222 us
  Pallas kernels  215 us (96%)
  local copies, waits for them, and re-layouts  5.45 us (2%)
    pallas_call x1, Pallas kernels, local(): pl.pallas_call(kernel, out_shape=(jax.ShapeDtypeStruct((OWNERS, COLS, HSH...  215 us

profile of v2, /device:TPU:1, one launch (start us, length us, event | category | flops | bytes accessed | tf_op | source)
XLA Modules:
  0.0 222.2 jit_solution(6934301348862026137)
XLA Ops:
  0.0 0.8 compare_reduce_fusion
  0.8 0.1 broadcast_in_dim.33
  0.9 0.1 broadcast_in_dim.34
  1.0 0.1 copy.11
  1.2 0.2 reduce_window_sum.13
  1.3 0.1 copy.12
  1.4 0.1 copy.13
  1.5 0.3 multiply_reduce_fusion
  1.8 0.1 copy.15
  1.9 0.2 broadcast_in_dim.37
  2.1 0.6 pad_bitcast_fusion.table
  2.7 215.4 %shard_map.46 = (bf16[64,112,256]{2,1,0:T(8,128)(2,1)}, bf16[16,768,1024]{2,1,0:T(8,128)(2,1)}) custom-call(bf16[128,7168]{1,0:T(8,128)(2,1)} %codes.1, f32[56,128]{1,0:T(8,128)} %bitcast.11, bf16[32,128]{1,0:T(8,128)(2,1)} %pad_bitcast_fusion.table, bf16[1,768,1024]{2,1,0:T(8,128)(2,1)} %grad.1), custom_call_target="tpu_custom_call" | custom-call | flops 11274289152 | bytes 100000000 | tf_op jit(solution)/shard_map/pallas_call | solution.py:474
  218.1 4.1 %copy.17 = bf16[64,112,256]{2,1,0:T(8,128)(2,1)} copy(bf16[64,112,256]{2,1,0:T(8,128)(2,1)} %get-tuple-element.6) | data formatting | bytes 7340032
  (8 shorter events, 0.1 us)

commit v3 on v2

--- a/solution.py
+++ b/solution.py
@@ -18,10 +18,12 @@
 WIDTH = NY * COLS
 SLOTS = OWNERS * CAP
 HSH = HW // NX
-TAB = 32
+TOPK = 8
+TAB = 16
 HALVES = 2
 PART = WIDTH // HALVES
 UNITS = RING * HALVES
+FIRST = 4
 DEPTH = 6
 KEEP = 4
 CUTS = 4
@@ -31,31 +33,13 @@
 F32 = jnp.float32
 
 
-def slot_table(routes):
-    targets = jnp.arange(OWNERS, dtype=jnp.int32) * EXP_DEV
-    member = jnp.any(routes[:, :, None] == targets[None, None, :], axis=1).astype(jnp.int32)
-    ranking = jnp.cumsum(member, axis=0) - member
-    slot_index = jnp.arange(CAP, dtype=jnp.int32)
-    selector = member.T[:, None, :] * (ranking.T[:, None, :] == slot_index[None, :, None]).astype(
-        jnp.int32
-    )
-    positions = jnp.arange(routes.shape[0], dtype=jnp.int32)
-    token = jnp.sum(selector * (positions[None, None, :] + 1), axis=2) - 1
-    token = token.reshape(NY, RING, 1, CAP)
-    place = lax.axis_index("expert") % QUAD
-    mine = (jnp.arange(QUAD, dtype=jnp.int32) == place)[None, None, :, None]
-    spread = jnp.where(mine, token, -1).reshape(NY, RING * QUAD * CAP // 128, 128)
-    spread = jnp.pad(spread, ((0, 0), (0, TAB // NY - spread.shape[1]), (0, 0)), constant_values=-1)
-    return spread.reshape(TAB, 128).astype(BF16)
-
-
 def rem(value, count):
     return lax.rem(value + count, count)
 
 
 def kernel(
-    codes, scales, table, grad, out, gbuf,
-    code, send0, send1, tok0, tok1, onehot, rows, gv, part, r1, r2, total,
+    codes, scales, ids, grad, out, gbuf,
+    code, send0, send1, tok0, tok1, ranks, onehot, rows, gv, part, r1, r2, total,
     il, ol, zs, zr, ys, yr, yfs, yfr, gs, gr, ss, sr, gl,
     s1s, s1r, s2s, s2r, cs, cr, cl,
 ):
@@ -134,49 +118,82 @@
     own_copies = [
         pltpu.make_async_copy(send[half].at[own], tok[half].at[me], ol.at[half]) for half in range(HALVES)
     ]
-    order = sorted(range(1, RING), key=lambda k: (min(k, RING - k), k))
+
+    def z_group(half, distance):
+        for chip in ([z] if distance == 0 else [z + distance, z - distance][:1 if distance == NZ // 2 else 2]):
+            for core in ([1 - c] if distance == 0 else [0, 1]):
+                target = 2 * rem(chip, NZ) + core
+                z_copy(half, rem(target - zc, RING), target, zc).start()
+
+    named = jnp.concatenate(
+        [ids[...].astype(F32), jnp.zeros((TAB - TOPK, TOK), F32)], axis=0
+    ).astype(BF16)
     for k in range(RING):
-        send0[k, PART:PART + TAB, :] = table[...]
+        send0[k, PART:PART + TAB, :] = named
+    def own_rows(h):
+        span = pl.ds(h * (SLOTS // 2), SLOTS // 2)
+        return rdma(grad.at[0, span], gbuf.at[own, span], ss.at[0, h], sr.at[0, h], x, sibling)
+
     for half in range(HALVES):
         restore(half)
         if half == 0:
             pl.semaphore_wait(barrier, RING - 1 + NY - 1 + 2)
-        for k in order:
-            z_copy(half, k, rem(zc + k, RING), zc).start()
+        for distance in range(NZ // 2 + 1):
+            z_group(half, distance)
         own_copies[half].start()
-
-    first_load = pltpu.make_async_copy(grad.at[0], gv.at[0], gl.at[0])
-    first_load.start()
+        if half == 0:
+            for h in range(2):
+                own_rows(h).start()
 
     def ring_z(j):
         return rem(z + (j + 1) // 2, NZ) if j % 2 else rem(z - j // 2, NZ)
 
-    def cut(ref, h):
-        return ref.at[pl.ds(h * (SLOTS // 2), SLOTS // 2)]
-
-    def ring_copy(j, h, src, index):
-        target = dev_down_z if j % 2 else dev_up_z
-        return rdma(cut(src, h), cut(gbuf.at[index], h), gs.at[j, h], gr.at[j, h], x, target)
-
-    def pair_copy(j, h, src, index):
-        return rdma(cut(src, h), cut(gbuf.at[index], h), ss.at[j, h], sr.at[j, h], x, sibling)
-
-    def holds(j, h):
-        return not (j == 7 and h == 0 or j == 8 and h == 1)
-
-    for h in range(2):
-        ring_copy(1, h, grad.at[0], own).start()
-        ring_copy(2, h, grad.at[0], own).start()
-        pair_copy(0, h, grad.at[0], own).start()
-
-    def ring_step(distance, h):
+    def cut(index, core, j):
+        size = SLOTS // 2
+        if j < 7:
+            return gbuf.at[index, pl.ds(core * size, size)]
+        return gbuf.at[index, pl.ds(core * size + (j % 2) * (size // 2), size // 2)]
+
+    def ring_copy(j, k, source):
+        ref = cut(2 * source + k, c, j)
+        return rdma(ref, ref, gs.at[j, k], gr.at[j, k], x, dev_down_z if j % 2 else dev_up_z)
+
+    def pair_copy(j, k, core):
+        ref = cut(2 * ring_z(j) + k, core, j)
+        return rdma(ref, ref, ss.at[j, k], sr.at[j, k], x, sibling)
+
+    def others_rows(h):
+        span = pl.ds(h * (SLOTS // 2), SLOTS // 2)
+        index = 2 * z + (1 - c)
+        return rdma(gbuf.at[index, span], gbuf.at[index, span], ss.at[0, h], sr.at[0, h], x, sibling)
+
+    def own_copy(j):
+        span = pl.ds(c * (SLOTS // 2), SLOTS // 2)
+        return rdma(
+            grad.at[0, span], gbuf.at[own, span], gs.at[j, c], gr.at[j, c],
+            x, dev_down_z if j % 2 else dev_up_z,
+        )
+
+    def issue(n):
+        distance, k = n // 2, n % 2
         for j in (2 * distance - 1, 2 * distance):
-            if holds(j, h):
-                index = 2 * ring_z(j) + c
-                ring_copy(j, h, gbuf.at[index], index).wait_recv()
-                if j <= 6 and holds(j + 2, h):
-                    ring_copy(j + 2, h, gbuf.at[index], index).start()
-                pair_copy(j, h, gbuf.at[index], index).start()
+            if n >= 2:
+                ring_copy(j + 2, k, ring_z(j)).start()
+                continue
+
+            @pl.when(c == k)
+            def _():
+                own_copy(j + 2).start()
+
+            @pl.when(c != k)
+            def _():
+                ring_copy(j + 2, k, z).start()
+
+    def arrive(n):
+        distance, k = n // 2 + 1, n % 2
+        for j in (2 * distance - 1, 2 * distance):
+            ring_copy(j, k, ring_z(j)).wait_recv()
+            pair_copy(j, k, c).start()
 
     def chunk(half, group, j):
         return tok[half].at[pl.ds(group * RING + 2 * ring_z(j), 2)]
@@ -190,8 +207,8 @@
         target = down_y if j % 2 else up_y
         return rdma(ref, ref, yfs.at[half, j], yfr.at[half, j], x, target * RING + zc)
 
-    def spread_y(half):
-        for j in range(NZ):
+    def spread_y(half, first, last):
+        for j in range(first, last):
             if j == 0:
                 own_copies[half].wait()
             for source in ([2 * z + (1 - c)] if j == 0 else [2 * ring_z(j), 2 * ring_z(j) + 1]):
@@ -205,25 +222,41 @@
             y_copy(half, 1, j, up_y, down_y).wait_recv()
             far_copy(half, j, up_y if j % 2 else down_y).start()
 
-    lane = lax.broadcasted_iota(jnp.int32, (128, 128), 1).astype(F32)
-
-    def gather(half, q):
+    before = jnp.where(
+        lax.broadcasted_iota(jnp.int32, (TOK, TOK), 0) < lax.broadcasted_iota(jnp.int32, (TOK, TOK), 1),
+        1.0, 0.0,
+    ).astype(BF16)
+    expert_id = (lax.broadcasted_iota(jnp.int32, (RING, TOK), 0) * EXP_DEV + y * (RING * EXP_DEV)).astype(F32)
+    slot_row = lax.broadcasted_iota(jnp.int32, (QUAD * CAP, TOK), 0).astype(F32)
+
+    def rank(q):
+        members = []
         for p in range(QUAD):
             words = tok0[QUAD * q + p, PART:PART + TAB, :].astype(F32)
-            each = TAB // NY
-            mine = words[0:each]
-            for group in range(1, NY):
-                mine = jnp.where(y == group, words[group * each:(group + 1) * each], mine)
-            for part_id in range(RING * QUAD * CAP // 128):
-                column = jnp.broadcast_to(mine[part_id:part_id + 1, :], (128, 128)).T
-                onehot[part_id * 128:(part_id + 1) * 128, p * 128:(p + 1) * 128] = jnp.where(
-                    column == lane, 1.0, 0.0
+            member = jnp.zeros((RING, TOK), F32)
+            for k in range(TOPK):
+                member = jnp.where(expert_id == words[k:k + 1, :], 1.0, member)
+            members.append(member)
+        member = jnp.concatenate(members, axis=0)
+        order = lax.dot_general(
+            member.astype(BF16), before, (((1,), (0,)), ((), ())), preferred_element_type=F32
+        )
+        ranks[q] = jnp.where(member > 0.5, order, -100.0)
+
+    def gather(half, q):
+        if half == 0:
+            rank(q)
+        height = QUAD * CAP
+        for p in range(QUAD):
+            for e in range(RING):
+                taken = ranks[q, p * RING + e:p * RING + e + 1, :]
+                onehot[e * height:(e + 1) * height, p * TOK:(p + 1) * TOK] = jnp.where(
+                    taken == slot_row - p * CAP, 1.0, 0.0
                 ).astype(BF16)
         blocks = jnp.concatenate([tok[half][QUAD * q + p, 0:PART, :] for p in range(QUAD)], axis=1)
         picked = lax.dot_general(
             onehot[...], blocks, (((1,), (1,)), ((), ())), preferred_element_type=F32
         ).astype(BF16)
-        height = QUAD * CAP
         for e in range(RING):
             rows[half, e, pl.ds(pl.multiple_of(q * height, height), height), :] = picked[
                 e * height:(e + 1) * height
@@ -233,40 +266,50 @@
 
     def gather_some(half, first, last):
         def body(step, carry):
-            group = rem(y + lax.div(step, quads) - 1, NY)
+            turn = lax.div(step, quads)
+            group = rem(y + jnp.where(turn == 3, 2, jnp.where(turn == 2, -1, turn)), NY)
             gather(half, group * quads + lax.rem(step, quads))
             return carry
 
         lax.fori_loop(first, last, body, 0)
 
+    def way(i):
+        past = jnp.maximum(i - 2, 0)
+        distance = jnp.where(i < 2, 0, lax.div(past, 4) + 1)
+        side = lax.rem(past, 2)
+        core = jnp.where(jnp.logical_or(i < 2, i == RING - 1), lax.rem(i, 2), lax.div(lax.rem(past, 4), 2))
+        return distance, side, core
+
     def place(i):
-        j = lax.div(i, 2)
-        half = lax.div(j + 1, 2)
-        zj = rem(jnp.where(lax.rem(j, 2) == 1, z + half, z - half + NZ), NZ)
-        core = rem(c + lax.rem(i, 2), 2)
-        return 2 * zj + core
+        distance, side, core = way(i)
+        return 2 * rem(jnp.where(side == 0, z + distance, z - distance + NZ), NZ) + core
 
     def unit(u):
-        i = jnp.where(u < 4, lax.rem(u, 2), lax.div(u, 2))
-        half = jnp.where(u < 4, lax.div(u, 2), lax.rem(u, 2))
+        early = u < 2 * FIRST
+        i = jnp.where(early, lax.rem(u, FIRST), lax.div(u, 2))
+        half = jnp.where(early, lax.div(u, FIRST), lax.rem(u, 2))
         return i, half
 
     def load(i):
-        return pltpu.make_async_copy(gbuf.at[place(i)], gv.at[lax.rem(i, 2)], gl.at[lax.rem(i, 2)])
+        slot = lax.rem(i, FIRST)
+        return pltpu.make_async_copy(gbuf.at[place(i)], gv.at[slot], gl.at[slot])
 
     def bring(i):
-        j = lax.div(i, 2)
+        distance, side, core = way(i)
         index = place(i)
-        other = lax.rem(i, 2) == 1
-        for h in range(2):
-            @pl.when(jnp.logical_and(other, j < NZ - 1))
-            def _():
-                ref = cut(gbuf.at[index], h)
-                rdma(ref, ref, ss.at[j, h], sr.at[j, h], x, sibling).wait_recv()
-
-            @pl.when(jnp.logical_and(other, j == NZ - 1))
-            def _():
-                pair_copy(8 - h, h, gbuf.at[index], index).wait_recv()
+        size = SLOTS // 2
+
+        @pl.when(distance < NZ // 2)
+        def _():
+            j = 2 * distance - 1 + side
+            ref = gbuf.at[index, pl.ds((1 - c) * size, size)]
+            rdma(ref, ref, ss.at[j, core], sr.at[j, core], x, sibling).wait_recv()
+
+        @pl.when(distance == NZ // 2)
+        def _():
+            for j in (7, 8):
+                ref = gbuf.at[index, pl.ds((1 - c) * size + (j % 2) * (size // 2), size // 2)]
+                rdma(ref, ref, ss.at[j, core], sr.at[j, core], x, sibling).wait_recv()
 
         load(i).start()
 
@@ -320,14 +363,14 @@
 
     def multiply(u):
         i, half = unit(u)
-        slot, held = lax.rem(u, DEPTH), lax.rem(i, 2)
+        slot, held = lax.rem(u, DEPTH), lax.rem(i, FIRST)
         expert = place(i)
 
         @pl.when(u >= DEPTH)
         def _():
             sent(u - DEPTH)
 
-        @pl.when(jnp.logical_or(u < 2, jnp.logical_and(u >= 4, lax.rem(u, 2) == 0)))
+        @pl.when(jnp.logical_or(u < FIRST, jnp.logical_and(u >= 2 * FIRST, lax.rem(u, 2) == 0)))
         def _():
             pltpu.make_async_copy(grad.at[0], gv.at[held], gl.at[held]).wait()
 
@@ -370,65 +413,86 @@
             ).astype(BF16)
         give(u)
 
-    def repeat(function):
+    def repeat(function, first):
         def body(u, carry):
             function(u)
             return carry
 
-        lax.fori_loop(0, 2, body, 0)
-
-    spread_y(0)
+        lax.fori_loop(first, first + 2, body, 0)
+
+    def far_y_arrived(half):
+        for j in range(NZ):
+            far_copy(half, j, far_y).wait_recv()
+
+    spread_y(0, 0, NZ)
+    for h in range(2):
+        others_rows(h).wait_recv()
+    for core in range(2):
+        @pl.when(c == core)
+        def _():
+            pltpu.make_async_copy(grad.at[0], gv.at[core], gl.at[core]).start()
+
+        @pl.when(c != core)
+        def _():
+            load(jnp.int32(core)).start()
+
+    issue(0)
+    issue(1)
+    gather_some(0, 0, quads)
     pass_y(0, 0, NZ)
-    spread_y(1)
-    gather_some(0, 0, 3 * quads)
-    for j in range(NZ):
-        far_copy(0, j, far_y).wait_recv()
+    gather_some(0, quads, 3 * quads)
+    spread_y(1, 0, NZ // 2)
+    far_y_arrived(0)
     gather_some(0, 3 * quads, 4 * quads)
-    bring(jnp.int32(1))
-    repeat(multiply)
+    repeat(multiply, 0)
+    spread_y(1, NZ // 2, NZ)
+    repeat(combine, 0)
     pass_y(1, 0, NZ // 2)
-    repeat(combine)
+    repeat(finish, 0)
+    gather_some(1, 0, quads)
+    arrive(0)
+    issue(2)
+    bring(jnp.int32(2))
+    bring(jnp.int32(3))
+    repeat(multiply, 2)
     pass_y(1, NZ // 2, NZ)
-    repeat(finish)
-    gather_some(1, 0, 3 * quads)
-    ring_step(1, 0)
-    for j in range(NZ):
-        far_copy(1, j, far_y).wait_recv()
+    repeat(combine, 2)
+    gather_some(1, quads, 3 * quads)
+    far_y_arrived(1)
     gather_some(1, 3 * quads, 4 * quads)
+    repeat(finish, 2)
 
     def main_step(u, carry):
-        following = lax.div(u, 2) + 1
-        due = jnp.logical_and(lax.rem(u, 2) == 1, following < RING)
-        fresh = lax.rem(following, 4) == 2
-
-        @pl.when(jnp.logical_and(due, jnp.logical_not(fresh)))
-        def _():
-            bring(following)
-
         @pl.when(u < UNITS)
         def _():
             multiply(u)
 
-        @pl.when(jnp.logical_and(u >= 4, u < UNITS + 2))
+        @pl.when(jnp.logical_and(u >= FIRST + 2, u < UNITS + 2))
         def _():
             combine(u - 2)
 
-        @pl.when(u >= 6)
+        @pl.when(u >= FIRST + 4)
         def _():
             finish(u - 4)
 
-        for at, distance, h in ((3, 1, 1), (9, 2, 0), (11, 2, 1), (17, 3, 0), (19, 3, 1), (26, 4, 0), (27, 4, 1)):
+        for n, at in ((1, 6), (2, 10), (3, 14), (4, 18), (5, 22), (6, 26), (7, 28)):
             @pl.when(u == at)
             def _():
-                ring_step(distance, h)
-
-        @pl.when(jnp.logical_and(due, fresh))
+                arrive(n)
+                if n + 2 < NZ:
+                    issue(n + 2)
+
+        following = lax.div(u, 2) + 1
+        odd = jnp.logical_and(lax.rem(following, 2) == 1, following < RING - 1)
+        due = jnp.where(odd, lax.rem(u, 2) == 0, lax.rem(u, 2) == 1)
+
+        @pl.when(jnp.logical_and(due, jnp.logical_and(following >= FIRST, following < RING)))
         def _():
             bring(following)
 
         return carry
 
-    lax.fori_loop(2, UNITS + 4, main_step, 0)
+    lax.fori_loop(FIRST, UNITS + 4, main_step, 0)
 
     def close(i, carry):
         for k in range(1, NY):
@@ -458,16 +522,14 @@
             y_copy(half, 0, j, y, up_y).wait_send()
             y_copy(half, 1, j, y, down_y).wait_send()
             far_copy(half, j, up_y if j % 2 else down_y).wait_send()
-    for j in range(0, 9):
-        for h in range(2):
-            if holds(j, h):
-                if j > 0:
-                    ring_copy(j, h, grad.at[0], own).wait_send()
-                pair_copy(j, h, grad.at[0], own).wait_send()
+    for k in range(2):
+        own_rows(k).wait_send()
+        for j in range(1, 9):
+            ring_copy(j, k, z).wait_send()
+            pair_copy(j, k, c).wait_send()
 
 
 def local(stash_codes, stash_scales, expert_ids, grad_rows):
-    table = slot_table(expert_ids)
     vmem = pl.BlockSpec(memory_space=pltpu.VMEM)
     hbm = pl.BlockSpec(memory_space=pl.ANY)
     dma = pltpu.SemaphoreType.DMA
@@ -485,9 +547,10 @@
             pltpu.VMEM((RING, PART, TOK), BF16),
             pltpu.VMEM((OWNERS, PART + TAB, TOK), BF16),
             pltpu.VMEM((OWNERS, PART, TOK), BF16),
+            pltpu.VMEM((OWNERS // QUAD, QUAD * RING, TOK), F32),
             pltpu.VMEM((RING * QUAD * CAP, QUAD * TOK), BF16),
             pltpu.VMEM((HALVES, RING, SLOTS, PART), BF16),
-            pltpu.VMEM((2, SLOTS, HW), BF16),
+            pltpu.VMEM((FIRST, SLOTS, HW), BF16),
             pltpu.VMEM((DEPTH, NX, PART, HSH), BF16),
             pltpu.VMEM((UNITS, 2, PART // 2, HSH), BF16),
             pltpu.VMEM((UNITS, 2, PART, HSH), BF16),
@@ -495,7 +558,7 @@
             dma((CUTS,)), dma((HALVES,)),
             dma((HALVES, RING)), dma((HALVES, RING)),
             dma((HALVES, 2, NZ)), dma((HALVES, 2, NZ)), dma((HALVES, NZ)), dma((HALVES, NZ)),
-            dma((9, 2)), dma((9, 2)), dma((9, 2)), dma((9, 2)), dma((2,)),
+            dma((9, 2)), dma((9, 2)), dma((9, 2)), dma((9, 2)), dma((FIRST,)),
             dma((UNITS, 2)), dma((UNITS, 2)), dma((UNITS, 2)), dma((UNITS, 2)),
             dma((KEEP, 2)), dma((RING, NY)), dma((KEEP,)),
         ],
@@ -505,7 +568,7 @@
         cost_estimate=pl.CostEstimate(
             flops=2 * SLOTS * D * HW, bytes_accessed=100_000_000, transcendentals=0
         ),
-    )(stash_codes, stash_scales.T, table, grad_rows)
+    )(stash_codes, stash_scales.T, expert_ids.T, grad_rows)
     return weight_grad
 
 

time: 225 us -> 209 us (0.929); the launches traced: 222 us -> 209 us
  Pallas kernels: 215 us -> 205 us
    pallas_call x1, Pallas kernels: 215 us -> 205 us  [local(): pl.pallas_call(kernel, out_shape=(jax.ShapeDtypeStruct((OWNERS, COLS, HSH...]
where the time goes in v3:
time: 209 us
  Pallas kernels  205 us (98%)
  local copies, waits for them, and re-layouts  4.11 us (2%)
    pallas_call x1, Pallas kernels, local(): pl.pallas_call(kernel, out_shape=(jax.ShapeDtypeStruct((OWNERS, COLS, HSH...  205 us

profile of v3, /device:TPU:1, one launch (start us, length us, event | category | flops | bytes accessed | tf_op | source)
XLA Modules:
  0.0 209.0 jit_solution(1001674994718778399)
XLA Ops:
  0.0 204.8 %shard_map.46 = (bf16[64,112,256]{2,1,0:T(8,128)(2,1)}, bf16[16,768,1024]{2,1,0:T(8,128)(2,1)}) custom-call(bf16[128,7168]{1,0:T(8,128)(2,1)} %codes.1, f32[56,128]{1,0:T(8,128)} %bitcast.2, s32[8,128]{1,0:T(8,128)} %bitcast.3, bf16[1,768,1024]{2,1,0:T(8,128)(2,1)} %grad.1), custom_call_target="tpu_custom_call" | custom-call | flops 11274289152 | bytes 100000000 | tf_op jit(solution)/shard_map/pallas_call | solution.py:536
  204.8 4.1 %copy.6 = bf16[64,112,256]{2,1,0:T(8,128)(2,1)} copy(bf16[64,112,256]{2,1,0:T(8,128)(2,1)} %get-tuple-element.6) | data formatting | bytes 7340032

commit v4 on v3

--- a/solution.py
+++ b/solution.py
@@ -536,11 +536,11 @@
     weight_grad, _ = pl.pallas_call(
         kernel,
         out_shape=(
-            jax.ShapeDtypeStruct((OWNERS, COLS, HSH), BF16),
+            pltpu.VMEM((OWNERS, COLS, HSH), BF16),
             jax.ShapeDtypeStruct((RING, SLOTS, HW), BF16),
         ),
         in_specs=[hbm, vmem, vmem, hbm],
-        out_specs=(hbm, hbm),
+        out_specs=(vmem, hbm),
         scratch_shapes=[
             pltpu.VMEM((TOK, D), BF16),
             pltpu.VMEM((RING, PART + TAB, TOK), BF16),
@@ -563,7 +563,7 @@
             dma((KEEP, 2)), dma((RING, NY)), dma((KEEP,)),
         ],
         compiler_params=pltpu.CompilerParams(
-            collective_id=0, has_side_effects=True, vmem_limit_bytes=58 * 1024 * 1024
+            collective_id=0, has_side_effects=True, vmem_limit_bytes=56 * 1024 * 1024
         ),
         cost_estimate=pl.CostEstimate(
             flops=2 * SLOTS * D * HW, bytes_accessed=100_000_000, transcendentals=0

time: 209 us -> 207 us (level)
  local copies, waits for them, and re-layouts: 4.11 us -> 1.84 us
    unnamed x1, local copies, waits for them, and re-layouts: 4.11 us -> 1.84 us
where the time goes in v4:
time: 207 us
  Pallas kernels  205 us (99%)
    pallas_call x1, Pallas kernels, local(): pl.pallas_call(kernel, out_shape=(pltpu.VMEM((OWNERS, COLS, HSH), BF16),...  205 us

profile of v4, /device:TPU:1, one launch (start us, length us, event | category | flops | bytes accessed | tf_op | source)
XLA Modules:
  0.0 206.6 jit_solution(138991615324623080)
XLA Ops:
  0.0 204.7 %shard_map.46 = (bf16[64,112,256]{2,1,0:T(8,128)(2,1)S(1)}, bf16[16,768,1024]{2,1,0:T(8,128)(2,1)}) custom-call(bf16[128,7168]{1,0:T(8,128)(2,1)} %codes.1, f32[56,128]{1,0:T(8,128)} %bitcast.2, s32[8,128]{1,0:T(8,128)} %bitcast.3, bf16[1,768,1024]{2,1,0:T(8,128)(2,1)} %grad.1), custom_call_target="tpu_custom_call" | custom-call | flops 11274289152 | bytes 100000000 | tf_op jit(solution)/shard_map/pallas_call | solution.py:536
  204.7 1.8 copy.6

commit v5 on v4

--- a/solution.py
+++ b/solution.py
@@ -462,38 +462,6 @@
     gather_some(1, 3 * quads, 4 * quads)
     repeat(finish, 2)
 
-    def main_step(u, carry):
-        @pl.when(u < UNITS)
-        def _():
-            multiply(u)
-
-        @pl.when(jnp.logical_and(u >= FIRST + 2, u < UNITS + 2))
-        def _():
-            combine(u - 2)
-
-        @pl.when(u >= FIRST + 4)
-        def _():
-            finish(u - 4)
-
-        for n, at in ((1, 6), (2, 10), (3, 14), (4, 18), (5, 22), (6, 26), (7, 28)):
-            @pl.when(u == at)
-            def _():
-                arrive(n)
-                if n + 2 < NZ:
-                    issue(n + 2)
-
-        following = lax.div(u, 2) + 1
-        odd = jnp.logical_and(lax.rem(following, 2) == 1, following < RING - 1)
-        due = jnp.where(odd, lax.rem(u, 2) == 0, lax.rem(u, 2) == 1)
-
-        @pl.when(jnp.logical_and(due, jnp.logical_and(following >= FIRST, following < RING)))
-        def _():
-            bring(following)
-
-        return carry
-
-    lax.fori_loop(FIRST, UNITS + 4, main_step, 0)
-
     def close(i, carry):
         for k in range(1, NY):
             source = rem(y - k, NY)
@@ -503,7 +471,64 @@
             ).wait_recv()
         return carry
 
-    lax.fori_loop(0, RING, close, 0)
+    def tokens_sent():
+        for half in range(HALVES):
+            for k in range(1, RING):
+                z_copy(half, k, rem(zc + k, RING), zc).wait_send()
+            for j in range(NZ):
+                y_copy(half, 0, j, y, up_y).wait_send()
+                y_copy(half, 1, j, y, down_y).wait_send()
+                far_copy(half, j, up_y if j % 2 else down_y).wait_send()
+
+    def shards_sent():
+        for k in range(2):
+            own_rows(k).wait_send()
+            for j in range(1, 9):
+                ring_copy(j, k, z).wait_send()
+                pair_copy(j, k, c).wait_send()
+
+    def main_step(u, carry):
+        @pl.when(u < UNITS)
+        def _():
+            multiply(u)
+
+        @pl.when(jnp.logical_and(u >= FIRST + 2, u < UNITS + 2))
+        def _():
+            combine(u - 2)
+
+        @pl.when(u == 2 * RING - 20)
+        def _():
+            tokens_sent()
+
+        @pl.when(u == UNITS + 1)
+        def _():
+            shards_sent()
+            lax.fori_loop(0, RING - 3, close, 0)
+
+        @pl.when(u >= FIRST + 4)
+        def _():
+            finish(u - 4)
+
+        for n, at in ((1, 7), (2, 11), (3, 15), (4, 19), (5, 23), (6, 27), (7, 29)):
+            @pl.when(u == at)
+            def _():
+                arrive(n)
+                if n + 2 < NZ:
+                    issue(n + 2)
+
+        following = lax.div(u, 2) + 1
+        odd = jnp.logical_and(lax.rem(following, 2) == 1, following < RING - 1)
+        due = jnp.where(odd, lax.rem(u, 2) == 0, lax.rem(u, 2) == 1)
+
+        @pl.when(jnp.logical_and(due, jnp.logical_and(following >= FIRST, following < RING)))
+        def _():
+            bring(following)
+
+        return carry
+
+    lax.fori_loop(FIRST, UNITS + 4, main_step, 0)
+
+    lax.fori_loop(RING - 3, RING, close, 0)
 
     def close_units(u, carry):
         sent(u)
@@ -515,18 +540,6 @@
 
     lax.fori_loop(UNITS - DEPTH, UNITS, close_units, 0)
     lax.fori_loop(UNITS - KEEP, UNITS, close_outs, 0)
-    for half in range(HALVES):
-        for k in range(1, RING):
-            z_copy(half, k, rem(zc + k, RING), zc).wait_send()
-        for j in range(NZ):
-            y_copy(half, 0, j, y, up_y).wait_send()
-            y_copy(half, 1, j, y, down_y).wait_send()
-            far_copy(half, j, up_y if j % 2 else down_y).wait_send()
-    for k in range(2):
-        own_rows(k).wait_send()
-        for j in range(1, 9):
-            ring_copy(j, k, z).wait_send()
-            pair_copy(j, k, c).wait_send()
 
 
 def local(stash_codes, stash_scales, expert_ids, grad_rows):

time: 207 us -> 206 us (level)
  no operation moved by 1% of the time
where the time goes in v5:
time: 206 us; the launch traced here: 205 us
  Pallas kernels  203 us (99%)
    pallas_call x1, Pallas kernels, local(): pl.pallas_call(kernel, out_shape=(pltpu.VMEM((OWNERS, COLS, HSH), BF16),...  203 us

profile of v5, /device:TPU:1, one launch (start us, length us, event | category | flops | bytes accessed | tf_op | source)
XLA Modules:
  0.0 204.8 jit_solution(6615665472418796946)
XLA Ops:
  0.0 202.9 %shard_map.46 = (bf16[64,112,256]{2,1,0:T(8,128)(2,1)S(1)}, bf16[16,768,1024]{2,1,0:T(8,128)(2,1)}) custom-call(bf16[128,7168]{1,0:T(8,128)(2,1)} %codes.1, f32[56,128]{1,0:T(8,128)} %bitcast.2, s32[8,128]{1,0:T(8,128)} %bitcast.3, bf16[1,768,1024]{2,1,0:T(8,128)(2,1)} %grad.1), custom_call_target="tpu_custom_call" | custom-call | flops 11274289152 | bytes 100000000 | tf_op jit(solution)/shard_map/pallas_call | solution.py:549
  202.9 1.8 copy.6

commit v6 on v5

--- a/solution.py
+++ b/solution.py
@@ -488,13 +488,13 @@
                 pair_copy(j, k, c).wait_send()
 
     def main_step(u, carry):
+        @pl.when(jnp.logical_and(u >= FIRST + 2, u < UNITS + 2))
+        def _():
+            combine(u - 2)
+
         @pl.when(u < UNITS)
         def _():
             multiply(u)
-
-        @pl.when(jnp.logical_and(u >= FIRST + 2, u < UNITS + 2))
-        def _():
-            combine(u - 2)
 
         @pl.when(u == 2 * RING - 20)
         def _():

time: 206 us -> 205 us (level)
  no operation moved by 1% of the time
where the time goes in v6:
time: 205 us
  Pallas kernels  203 us (99%)
    pallas_call x1, Pallas kernels, local(): pl.pallas_call(kernel, out_shape=(pltpu.VMEM((OWNERS, COLS, HSH), BF16),...  203 us

profile of v6, /device:TPU:1, one launch (start us, length us, event | category | flops | bytes accessed | tf_op | source)
XLA Modules:
  0.0 204.7 jit_solution(1630325164124474702)
XLA Ops:
  0.0 202.8 %shard_map.46 = (bf16[64,112,256]{2,1,0:T(8,128)(2,1)S(1)}, bf16[16,768,1024]{2,1,0:T(8,128)(2,1)}) custom-call(bf16[128,7168]{1,0:T(8,128)(2,1)} %codes.1, f32[56,128]{1,0:T(8,128)} %bitcast.2, s32[8,128]{1,0:T(8,128)} %bitcast.3, bf16[1,768,1024]{2,1,0:T(8,128)(2,1)} %grad.1), custom_call_target="tpu_custom_call" | custom-call | flops 11274289152 | bytes 100000000 | tf_op jit(solution)/shard_map/pallas_call | solution.py:549
  202.8 1.8 copy.6
